TPU v7x, 128 devices: a whole 4x4x4 slice. The times are simulated.
128 devices in a mesh: dp: 32 (over x, z, y_lo), tensor: 4 (over y_hi, core).
Axes of the slice: x: 4, y: 4 (y_hi: 2, y_lo: 2; y = y_hi * 2 + y_lo), z: 4, core: 2. Of those that a mesh axis runs over, the one named last changes fastest.
Arguments:
- entering_activations: bfloat16 [32768, 768], P('dp'), may hold values from -6 to 6
- sample_sizes: int32 [32, 16], P('dp'), may hold values from 0 to 1024, as said below
- initial_layernorm_scale: float32 [768], replicated, may hold values from 0.5 to 1.5
- initial_layernorm_offset: float32 [768], replicated, may hold values from -3 to 3
- temporal_lookup_fraction: float32 [768], replicated, may hold values from 0 to 1
- temporal_content_fraction: float32 [768], replicated, may hold values from 0 to 1
- temporal_gating_fraction: float32 [768], replicated, may hold values from 0 to 1
- fading_speed_logarithm: float32 [768], replicated, may hold values from -9 to -1.5
- present_reward: float32 [768], replicated, may hold values from -1 to 1
- temporal_gating_matrix: bfloat16 [768, 768], replicated, may hold values from -0.21875 to 0.21875
- temporal_lookup_matrix: bfloat16 [768, 768], replicated, may hold values from -0.21875 to 0.21875
- temporal_content_matrix: bfloat16 [768, 768], replicated, may hold values from -0.21875 to 0.21875
- temporal_emission_matrix: bfloat16 [768, 768], replicated, may hold values from -0.875 to 0.875
- latter_layernorm_scale: float32 [768], replicated, may hold values from 0.5 to 1.5
- latter_layernorm_offset: float32 [768], replicated, may hold values from -3 to 3
- feedforward_lookup_fraction: float32 [768], replicated, may hold values from 0 to 1
- feedforward_gating_fraction: float32 [768], replicated, may hold values from 0 to 1
- feedforward_gating_matrix: bfloat16 [768, 768], replicated, may hold values from -0.21875 to 0.21875
- feedforward_lookup_matrix: bfloat16 [768, 3072], P(None, 'tensor'), may hold values from -0.21875 to 0.21875
- feedforward_content_matrix: bfloat16 [3072, 768], P('tensor'), may hold values from -0.109375 to 0.109375
- upstream_adjoint: bfloat16 [32768, 768], P('dp'), may hold values from -6 to 6
Outputs:
- out: bfloat16 [32768, 768], P('dp')
- grad_inputs: float32 [32768, 768], P('dp')
- grad_norm1_gain: float32 [768], replicated
- grad_norm1_bias: float32 [768], replicated
- grad_mix_key: float32 [768], replicated
- grad_mix_value: float32 [768], replicated
- grad_mix_recept: float32 [768], replicated
- gradient_log_decay: float32 [768], replicated
- present_reward_derivative: float32 [768], replicated
- grad_recept_weight: float32 [768, 768], replicated
- grad_key_weight: float32 [768, 768], replicated
- grad_value_weight: float32 [768, 768], replicated
- grad_output_weight: float32 [768, 768], replicated
- grad_norm2_gain: float32 [768], replicated
- grad_norm2_bias: float32 [768], replicated
- grad_chan_mix_key: float32 [768], replicated
- grad_chan_mix_recept: float32 [768], replicated
- grad_chan_recept: float32 [768, 768], replicated
- grad_chan_key: float32 [768, 3072], P(None, 'tensor')
- grad_chan_value: float32 [3072, 768], P('tensor')
Inputs may be any that keep to these rules, and one draw needn't show every extreme that they name: `sample_sizes`: row g lists, in order from position 0, the lengths of the sequences packed into the 1024 positions of data device g. Every length is a multiple of 64; nonzero lengths come first, and their sum lies between 512 and 1024; positions after it are padding. On one device, drawn from the seed, a single sequence fills all 1024 positions.
All inputs are finite; a program needn't handle non-finite values.
Results may differ from a plain program's by a relative error of at most 0.0095.
Values sent between devices are 32-bit elements; how exact they have to be, the bound alone decides.
A program may use at most 192 MiB of HBM per device.

v0:
```python
import functools

import jax
import jax.numpy as jnp
from jax import lax
from jax.experimental import pallas as pl
from jax.experimental.pallas import tpu as pltpu
from jax.sharding import PartitionSpec as P

F32 = jnp.float32
BF16 = jnp.bfloat16
EPSILON = 1e-05
SEG = 64
D = 768
T = 1024
HALF = 512
HALF_D = D // 2
BLK = 512
SUB = 32
NSEG = T // SEG
PER = HALF // BLK
SLOTS = PER


def nn(left, right):
    return jnp.dot(left, right, preferred_element_type=F32)


def nt(left, right):
    return lax.dot_general(left, right, (((1,), (1,)), ((), ())), preferred_element_type=F32)


def tn(left, right):
    return lax.dot_general(left, right, (((0,), (0,)), ((), ())), preferred_element_type=F32)


def normalize(v):
    c = v - jnp.mean(v, axis=-1, keepdims=True)
    r = lax.rsqrt(jnp.mean(c * c, axis=-1, keepdims=True) + EPSILON)
    return c * r, r


def roll_down(v, first):
    row = lax.broadcasted_iota(jnp.int32, v.shape, 0)
    return jnp.where(row == 0, first, pltpu.roll(v, 1, 0))


def two_parts(v):
    hi = v.astype(BF16)
    return hi, (v - hi.astype(F32)).astype(BF16)


def triangle(upper):
    row = lax.broadcasted_iota(jnp.int32, (SEG, 2 * SEG), 0)
    col = lax.broadcasted_iota(jnp.int32, (SEG, 2 * SEG), 1)
    col = jnp.where(col >= SEG, col - SEG, col)
    keep = (col > row) if upper else (col < row)
    return jnp.where(keep, 1.0, 0.0).astype(BF16)


def running(tri, first, second):
    both = jnp.concatenate([first, second], axis=1)
    hi, lo = two_parts(both)
    return nn(tri, jnp.concatenate([hi, lo], axis=0)), both


def decay_tables(dec, rise, fade):
    rate = jnp.exp(dec)
    offs = lax.broadcasted_iota(jnp.int32, (SEG, D), 0).astype(F32)
    rise[...] = jnp.exp((offs + 1.0) * rate)
    fade[...] = jnp.exp(-offs * rate)
    return jnp.exp(-float(SEG) * rate)


def spread(dst, first, v):
    for s in range(v.shape[0] // SEG):
        dst[2 * SEG * s + first : 2 * SEG * s + first + SEG, :] = v[SEG * s : SEG * (s + 1), :]


def front_kernel(
    half_ref, len_ref, x_ref, adj_ref, g1_h, b1_h, fk_h, fv_h, fr_h, dec_h, rew_h, g2_h, b2_h, ck_h, cr_h,
    wr_h, wk_h, wv_h, wo_h, wg_h, wfk_h, wfv_h,
    flags, pq, grads, n1_h, dh1_h, a_h, v_h, sr_h, w_h, rd_h, sn_h, sd_h, after_h, gate_h, n2_h, dh2_h,
    r1_h, r2_h, keyed_h, valued_h, recepted_h, mixed_h, chrec_h,
    wr, wk, wv, wo, wg, wfk, wfv, wide, narrow, low, gbuf,
    rise, fade, through, expu, nc, dc, p1, p2, kb, vb, rb, hb, cks, hid, gch, gpr, pv, win, outs, gsem,
):
    i = pl.program_id(0)
    slot = lax.rem(i, SLOTS)
    given = (g1_h, b1_h, fk_h, fv_h, fr_h, dec_h, rew_h, g2_h, b2_h, ck_h, cr_h)
    g1, b1, fk, fv, fr, dec, rew, g2, b2, ck, cr = (pv.at[k : k + 1, :] for k in range(len(given)))
    n1_o, dh1_o, a_o, v_o, sr_o, w_o, rd_o, sn_o, sd_o, after_o, gate_o, n2_o, dh2_o = (
        wide.at[slot, k] for k in range(13)
    )
    r1_o, r2_o = (narrow.at[slot, k] for k in range(2))
    keyed_o, valued_o, recepted_o, mixed_o, chrec_o = (low.at[slot, k] for k in range(5))
    loads = [
        pltpu.make_async_copy(src, dst, win.at[k])
        for k, (src, dst) in enumerate(
            ((wk_h, wk), (wv_h, wv), (wr_h, wr), (wo_h, wo), (wfk_h, wfk), (wg_h, wg), (wfv_h, wfv))
        )
    ]
    kept = pl.ds(pl.multiple_of(lax.rem(i, PER) * BLK, BLK), BLK)
    held = (
        (wide, 0, n1_h), (wide, 1, dh1_h), (narrow, 0, r1_h), (low, 0, keyed_h), (low, 1, valued_h), (low, 2, recepted_h),
        (wide, 2, a_h), (wide, 3, v_h), (wide, 4, sr_h), (wide, 5, w_h), (wide, 6, rd_h), (wide, 7, sn_h),
        (wide, 8, sd_h), (low, 3, mixed_h),
        (wide, 9, after_h), (wide, 11, n2_h), (wide, 12, dh2_h), (narrow, 1, r2_h), (low, 4, chrec_h),
        (wide, 10, gate_h),
    )

    def saves(at):
        return [
            pltpu.make_async_copy(src.at[at, n], dst.at[kept, :], outs.at[at, k])
            for k, (src, n, dst) in enumerate(held)
        ]

    def save(lo, hi):
        @pl.when(i // PER == half_ref[0])
        def _():
            for copy in saves(slot)[lo:hi]:
                copy.start()

    def loaded(lo, hi):
        @pl.when(i == 0)
        def _():
            for copy in loads[lo:hi]:
                copy.wait()

    @pl.when(i == 0)
    def _():
        for copy in loads:
            copy.start()

    def reuse(lo, hi):
        @pl.when((i >= PER) & (half_ref[0] == 0))
        def _():
            for copy in saves(slot)[lo:hi]:
                copy.wait()

    reuse(0, 6)
    @pl.when(i == 0)
    def _():
        for b in range(NSEG):
            flags[0, b] = 0.0
        begin = jnp.int32(0)
        for j in range(NSEG):
            size = len_ref[0, j]
            at = lax.shift_right_logical(begin, 6)

            @pl.when(size > 0)
            def _():
                flags[0, at] = 1.0

            begin = begin + size
        for b in range(NSEG):
            flags[1, b] = jnp.where(b * SEG < begin, 1.0, 0.0)
        for k, v in enumerate(given):
            pv[k : k + 1, :] = v[...].reshape(1, D)
        through[...] = decay_tables(dec[...], rise, fade)
        expu[...] = jnp.exp(rew[...])
        nc[...] = jnp.zeros_like(nc)
        dc[...] = jnp.zeros_like(dc)
        p1[...] = jnp.zeros_like(p1)
        p2[...] = jnp.zeros_like(p2)

    fresh = [flags[0, i * (BLK // SEG) + s] for s in range(BLK // SEG)]
    live = [flags[1, i * (BLK // SEG) + s] for s in range(BLK // SEG)]

    for s in range(BLK // SUB):
        at = pl.ds(s * SUB, SUB)
        n1, r1 = normalize(x_ref[at, :].astype(F32))
        h1 = n1 * g1[...] + b1[...]
        before = p1[...]
        if (s * SUB) % SEG == 0:
            before = before * (1.0 - fresh[s * SUB // SEG])
        sh = roll_down(h1, before)
        p1[...] = h1[SUB - 1 :, :]
        dh1 = h1 - sh
        keyed_o[at, :] = (sh + dh1 * fk[...]).astype(BF16)
        valued_o[at, :] = (sh + dh1 * fv[...]).astype(BF16)
        recepted_o[at, :] = (sh + dh1 * fr[...]).astype(BF16)
        n1_o[at, :] = n1
        dh1_o[at, :] = dh1
        r1_o[at, :] = jnp.broadcast_to(r1, (SUB, 128))

    save(0, 6)
    reuse(6, 14)
    loaded(0, 3)
    kb[...] = nn(keyed_o[...], wk[...])
    vb[...] = nn(valued_o[...], wv[...])
    rb[...] = nn(recepted_o[...], wr[...])

    tri = triangle(False)
    for s in range(BLK // SEG):
        at = pl.ds(s * SEG, SEG)
        keep = 1.0 - fresh[s]
        for c in range(D // 128):
            cols = pl.ds(c * 128, 128)
            a = jnp.exp(kb[at, cols])
            v = vb[at, cols]
            lift = rise[:, cols] * a
            cum, both = running(tri, lift * v, lift)
            ncar = nc[:, cols] * keep
            dcar = dc[:, cols] * keep
            sn = fade[:, cols] * (ncar + cum[:, :128])
            sd = fade[:, cols] * (dcar + cum[:, 128:])
            th = through[:, cols]
            nc[:, cols] = th * (ncar + (cum[SEG - 1 :, :128] + both[SEG - 1 :, :128]))
            dc[:, cols] = th * (dcar + (cum[SEG - 1 :, 128:] + both[SEG - 1 :, 128:]))
            e = expu[:, cols] * a
            rd = 1.0 / (sd + e)
            w = (sn + e * v) * rd
            sr = jax.nn.sigmoid(rb[at, cols])
            mixed_o[at, cols] = (sr * w).astype(BF16)

            a_o[at, cols] = a
            v_o[at, cols] = v
            sr_o[at, cols] = sr
            w_o[at, cols] = w
            rd_o[at, cols] = rd
            sn_o[at, cols] = sn
            sd_o[at, cols] = sd

    save(6, 14)
    reuse(14, 20)
    loaded(3, 4)
    hb[...] = nn(mixed_o[...], wo[...])

    rows0 = pl.multiple_of(i * BLK, BLK)
    for s in range(BLK // SUB):
        at = pl.ds(s * SUB, SUB)
        after = x_ref[at, :].astype(F32) + hb[at, :]
        n2, r2 = normalize(after)
        h2 = n2 * g2[...] + b2[...]
        before = p2[...]
        if (s * SUB) % SEG == 0:
            before = before * (1.0 - fresh[s * SUB // SEG])
        sh = roll_down(h2, before)
        p2[...] = h2[SUB - 1 :, :]
        dh2 = h2 - sh
        cks[pl.ds(rows0 + s * SUB, SUB), :] = (sh + dh2 * ck[...]).astype(BF16)
        chrec_o[at, :] = (sh + dh2 * cr[...]).astype(BF16)
        after_o[at, :] = after
        n2_o[at, :] = n2
        dh2_o[at, :] = dh2
        r2_o[at, :] = jnp.broadcast_to(r2, (SUB, 128))

    save(14, 19)
    loaded(4, 7)
    rows = pl.ds(rows0, BLK)
    hb[...] = nn(cks[rows, :], wfk[...])
    gate_o[...] = nn(chrec_o[...], wg[...])
    for s in range(BLK // SUB):
        at = pl.ds(s * SUB, SUB)
        hp = jnp.maximum(hb[at, :], 0.0)
        hid[pl.ds(rows0 + s * SUB, SUB), :] = (hp * hp).astype(BF16)
        gate = jax.nn.sigmoid(gate_o[at, :])
        gate_o[at, :] = gate
        go = adj_ref[at, :].astype(F32) * live[s * SUB // SEG]
        gch[pl.ds(rows0 + s * SUB, SUB), :] = (go * gate).astype(BF16)
    save(19, 20)
    spread(pq, 0, nn(hid[rows, :], wfv[...]))
    kb[...] = nt(gch[rows, :], wfv[...])
    for s in range(BLK // SUB):
        at = pl.ds(s * SUB, SUB)
        gpr[pl.ds(rows0 + s * SUB, SUB), :] = (2.0 * jnp.maximum(hb[at, :], 0.0) * kb[at, :]).astype(BF16)
    spread(pq, SEG, nt(gpr[rows, :], wfk[...]))

    @pl.when(i == T // BLK - 1)
    def _():
        out_copies = []
        for k, (left, right) in enumerate(((cks, gpr), (hid, gch))):
            for c in range(D // 256):
                at = pl.ds(D * k + 256 * c, 256)
                gbuf[at, :] = tn(left[:, pl.ds(256 * c, 256)], right[...])
                out_copies.append(pltpu.make_async_copy(gbuf.at[at, :], grads.at[at, :], gsem.at[3 * k + c]))
                out_copies[-1].start()
        for copy in out_copies:
            copy.wait()

    @pl.when((i == T // BLK - 1) & (half_ref[0] == 1))
    def _():
        for s in range(SLOTS):
            for copy in saves(s):
                copy.wait()


def front(half, sizes, x, adj, vecs, mats):
    steps = T // BLK
    blk = lambda w: pl.BlockSpec((BLK, w), lambda i, h: (i, 0))
    vec = pl.BlockSpec((D,), lambda i, h: (0,))
    anywhere = pl.BlockSpec(memory_space=pl.ANY)
    sds = jax.ShapeDtypeStruct
    vm = pltpu.VMEM
    return pl.pallas_call(
        front_kernel,
        grid_spec=pltpu.PrefetchScalarGridSpec(
            num_scalar_prefetch=1,
            grid=(steps,),
            in_specs=[pl.BlockSpec(memory_space=pltpu.SMEM), blk(D), blk(D)] + [vec] * 11 + [anywhere] * 7,
            out_specs=[pl.BlockSpec(memory_space=pltpu.SMEM), pl.BlockSpec((2 * BLK, D), lambda i, h: (i, 0))]
            + [anywhere] * 21,
            scratch_shapes=[vm((D, D), BF16)] * 7
            + [vm((SLOTS, 13, BLK, D), F32), vm((SLOTS, 2, BLK, 128), F32), vm((SLOTS, 5, BLK, D), BF16), vm((2 * D, D), F32)]
            + [vm((SEG, D), F32)] * 2 + [vm((1, D), F32)] * 6 + [vm((BLK, D), F32)] * 4
            + [vm((T, D), BF16)] * 4 + [vm((16, D), F32)]
            + [pltpu.SemaphoreType.DMA((7,)), pltpu.SemaphoreType.DMA((SLOTS, 20)), pltpu.SemaphoreType.DMA((6,))],
        ),
        out_shape=[sds((2, NSEG), F32), sds((2 * T, D), F32), sds((2 * D, D), F32)]
        + [sds((HALF, D), F32)] * 13 + [sds((HALF, 128), F32)] * 2 + [sds((HALF, D), BF16)] * 5,
        compiler_params=pltpu.CompilerParams(dimension_semantics=("arbitrary",), vmem_limit_bytes=62 * 2**20),
        cost_estimate=pl.CostEstimate(flops=11 * 2 * T * D * D, bytes_accessed=60 * 2**20, transcendentals=4 * T * D),
        name="front",
    )(half, sizes, x, adj, *vecs, *mats)


MESH = pl.DeviceIdType.MESH
COPIES = 256
FF_ROWS = 2 * D
R_ROWS = 2048
MATS = 5
BACK_VMEM = 39
FINISH_VMEM = 2
SETTLE = 24
ORDER = (
    "cbBaBMdbBBaBcdBMabdcabdcBabBdMMcMaMbMMdcMOMMbMMO",
    "OcMMpqMMMMMsMtpqrOMOMMMtpsrqMGptrsdaOOqrtsVpqdtV",
    "OrGsqGcptGGasrpbqtrsGVpGqtOsGrGV",
)
NVEC = 11


def rows(start, size):
    return pl.ds(pl.multiple_of(start, 8), size)


def each(count, step, body, reverse=False):
    def run(k, carry):
        body((count - 1 - k) * step if reverse else k * step)
        return carry

    lax.fori_loop(0, count, run, 0)


class Links:
    def __init__(self, sends, recvs):
        self.sends, self.recvs, self.used, self.open, self.step = sends, recvs, 0, [], 0

    def send(self, src, dst, device):
        k = self.used
        self.used += 1
        copy = pltpu.make_async_remote_copy(
            src_ref=src, dst_ref=dst, send_sem=self.sends.at[k], recv_sem=self.recvs.at[k],
            device_id=device, device_id_type=MESH,
        )
        copy.start()
        self.open.append((self.step, copy))
        return copy

    def sent(self, copy):
        if all(kept[1] is not copy for kept in self.open):
            return
        self.open = [kept for kept in self.open if kept[1] is not copy]
        copy.wait_send()

    def settle(self, steps):
        while self.open and self.open[0][0] < self.step - steps:
            self.open.pop(0)[1].wait_send()
        self.step += 1

    def finish(self):
        for _, copy in self.open:
            copy.wait_send()


def add_into(dst, dst_at, terms, size, step=16):
    if size % step:
        step = 8

    def body(r):
        total = dst[rows(dst_at + r, step), :]
        for ref, start in terms:
            total = total + ref[rows(start + r, step), :]
        dst[rows(dst_at + r, step), :] = total

    each(size // step, step, body)


def ring_reduce(links, data, base, size, place, up, down, land, land_at, source, loaded):
    s = size // 4
    qa = (s // 2 + 7) // 8 * 8
    qb = s - qa
    mine = base + place * s
    nxt = base + lax.rem(place + 1, 4) * s
    opp = base + lax.rem(place + 2, 4) * s
    prv = base + lax.rem(place + 3, 4) * s
    starts = [land_at]
    for size_k in (qa, qb, qb, qa, qa, qb):
        starts.append(starts[-1] + size_k)
    spot = [land.at[pl.ds(a, b - a), :] for a, b in zip(starts, starts[1:])]
    fwd_a = links.send(source.at[rows(opp, qa), :], spot[0], up)
    fwd_b = links.send(source.at[rows(opp + qa, qb), :], spot[1], down)
    dir_b = links.send(source.at[rows(nxt + qa, qb), :], spot[2], up)
    dir_a = links.send(source.at[rows(prv, qa), :], spot[3], down)
    yield
    if loaded is not None:
        loaded()
    fwd_a.wait_recv()
    add_into(land, starts[0], [(data, nxt)], qa)
    cmb_a = links.send(spot[0], spot[4], up)
    fwd_b.wait_recv()
    add_into(land, starts[1], [(data, prv + qa)], qb)
    for copy in (fwd_a, fwd_b, dir_b, dir_a):
        links.sent(copy)
    cmb_b = links.send(spot[1], spot[5], down)
    yield
    dir_a.wait_recv()
    dir_b.wait_recv()
    cmb_a.wait_recv()
    cmb_b.wait_recv()
    add_into(data, mine, [(land, starts[3]), (land, starts[4])], qa)
    add_into(data, mine + qa, [(land, starts[2]), (land, starts[5])], qb)


def ring_gather(links, data, base, size, place, up, down, share):
    s = size // 4
    qa = (s // 2 + 7) // 8 * 8
    qb = s - qa
    mine = base + place * s
    nxt = base + lax.rem(place + 1, 4) * s
    opp = base + lax.rem(place + 2, 4) * s
    prv = base + lax.rem(place + 3, 4) * s
    own = data.at[rows(mine, s), :]
    to_up = links.send(own, own, up)
    to_down = links.send(own, own, down)
    share(own)
    yield
    to_up.wait_recv()
    half_a = data.at[rows(prv, qa), :]
    on_a = links.send(half_a, half_a, up)
    to_down.wait_recv()
    half_b = data.at[rows(nxt + qa, qb), :]
    on_b = links.send(half_b, half_b, down)
    share(data.at[rows(prv, s), :])
    share(data.at[rows(nxt, s), :])
    yield
    on_a.wait_recv()
    on_b.wait_recv()
    share(data.at[rows(opp, s), :])


def near_reduce(links, data, base, size, place, others, land, land_at, stage_at):
    s = size // 4
    copies = []
    for k, device in enumerate(others):
        theirs = base + lax.rem(place + 1 + k, 4) * s
        stage = stage_at + k * s

        def body(r, theirs=theirs, stage=stage):
            land[rows(stage + r, 8), :] = data[rows(theirs + r, 8), :]

        each(s // 8, 8, body)
        copies.append(links.send(land.at[pl.ds(stage, s), :], land.at[pl.ds(land_at + k * s, s), :], device))
    yield
    for copy in copies:
        copy.wait_recv()
    add_into(data, base + place * s, [(land, land_at + k * s) for k in range(3)], s, 8)


def near_gather(links, data, base, size, place, others):
    s = size // 4
    own = data.at[rows(base + place * s, s), :]
    copies = [links.send(own, own, device) for device in others]
    yield
    for copy in copies:
        copy.wait_recv()


def sum_of_four(links, data, base, size, place, others, land, land_at):
    mine = rows(land_at + place * size, size)
    land[mine, :] = data[rows(base, size), :]
    copies = [links.send(land.at[mine, :], land.at[mine, :], device) for device in others]
    yield
    for copy in copies:
        copy.wait_recv()

    def body(r):
        a, b, c, d = (land[rows(land_at + k * size + r, 8), :] for k in range(4))
        data[rows(base + r, 8), :] = (a + b) + (c + d)

    each(size // 8, 8, body)


def all_reduce(links, data, base, size, axes, land, land_at, last, last_land, last_at, source, loaded, share):
    (place, up, _, down), (place_2, *others) = axes
    yield from ring_reduce(links, data, base, size, place, up, down, land, land_at, source, loaded)
    part = size // 4
    at = base + place * part
    yield from near_reduce(links, data, at, part, place_2, others, land, land_at + 3 * part, land_at + part)
    yield from last(links, data, at + place_2 * (part // 4), part // 4, last_land, last_at)
    yield from near_gather(links, data, at, part, place_2, others)
    yield from ring_gather(links, data, base, size, place, up, down, share)


def back_kernel(
    flags, pq, grads, n1_h, dh1_h, a_h, v_h, sr_h, w_h, rd_h, sn_h, sd_h, after_h, gate_h, n2_h, dh2_h,
    r1_h, r2_h, keyed_h, valued_h, recepted_h, mixed_h, chrec_h, adj_h,
    g1_h, fk_h, fv_h, fr_h, dec_h, rew_h, g2_h, ck_h, cr_h, wr_h, wk_h, wv_h, wo_h, wg_h,
    out_o, gi, vec_o, red, ff,
    front4, r1, r2, keyed, valued, recepted, mixed, chrec, adj, wr, wo, wg,
    fin, xb, gg, gb, gk, gv, gp, t0, t1, t2, other, ffland, yland, vland,
    urow, urow2, gsend, grecv, acc, rise, fade, through, expu, sums, gc, pv,
    sends, recvs, fill, ready_ring, ready_sib,
):
    dp = lax.axis_index("dp")
    tensor = lax.axis_index("tensor")
    x, z, yl = dp // 8, lax.rem(dp // 2, 4), lax.rem(dp, 2)
    h, c = tensor // 2, lax.rem(tensor, 2)
    y = 2 * h + yl

    def chip(cx, cz, cy):
        cx, cz, cy = lax.rem(cx + 4, 4), lax.rem(cz + 4, 4), lax.rem(cy + 4, 4)
        return {"dp": (cx * 4 + cz) * 2 + lax.rem(cy, 2), "tensor": (cy // 2) * 2 + c}

    xp, xo, xm = (chip(x + k, z, y) for k in (1, 2, 3))
    zp, zo, zm = (chip(x, z + k, y) for k in (1, 2, 3))
    yp, opp, ym = (chip(x, z, y + k) for k in (1, 2, 3))
    sib = {"dp": dp, "tensor": h * 2 + (1 - c)}
    pair = {"dp": dp + 1 - 2 * yl, "tensor": tensor}
    own_at, other_at = h * HALF, (1 - h) * HALF
    mine_at = c * R_ROWS

    given = (g1_h, fk_h, fv_h, fr_h, dec_h, rew_h, g2_h, ck_h, cr_h)
    g1, fk, fv, fr, dec, rew, g2, ck, cr = (pv.at[k : k + 1, :] for k in range(len(given)))
    barrier = pltpu.get_barrier_semaphore()
    partners = (xp, xo, xm, zp, zo, zm, yp, ym, opp, sib)
    for device in partners:
        pl.semaphore_signal(barrier, inc=1, device_id=device, device_id_type=MESH)

    fills = []

    def bring(src, dst):
        copy = pltpu.make_async_copy(src, dst, fill.at[len(fills)])
        copy.start()
        fills.append(copy)
        return copy

    def group(start):
        return rows(2 * start, 2 * SEG)

    PART, ARECV, CRECV, BRECV = (512 * k for k in range(4))
    part_in = [
        bring(pq.at[group(other_at + 128 * j + SEG * c), :], xb.at[pl.ds(PART + 128 * j, 128), :]) for j in range(4)
    ]
    ff_in = bring(grads, ff)
    fin_in = [
        bring(pq.at[group(own_at + 128 * j + SEG * c), :], fin.at[group(128 * j + SEG * c), :]) for j in range(4)
    ]
    pl.semaphore_wait(barrier, len(partners))

    links = Links(sends, recvs)
    ax, az, ay = (x, xp, xo, xm), (z, zp, zo, zm), (y, yp, opp, ym)

    def with_pair(links, data, base, size, land, land_at):
        whole = data.at[rows(base, size), :]
        copy = links.send(whole, land.at[pl.ds(land_at, size), :], pair)
        yield
        links.sent(copy)
        copy.wait_recv()
        add_into(data, base, [(land, land_at)], size, 8)

    def with_ring(axis):
        def last(links, data, base, size, land, land_at):
            yield from sum_of_four(links, data, base, size, axis[0], axis[1:], land, land_at)

        return last

    waited = []

    def ff_loaded():
        if not waited:
            ff_in.wait()
            waited.append(True)

    n = FF_ROWS // 4
    ffs = [
        all_reduce(
            links, ff, n * k, n, (ax, az) if k % 2 == 0 else (az, ax), ffland, n * k,
            with_pair, ffland, n * k + 15 * n // 16, grads, ff_loaded, lambda ref: None,
        )
        for k in range(4)
    ]

    a_in = [
        links.send(pq.at[group(other_at + 128 * j + SEG * (1 - c)), :], xb.at[pl.ds(ARECV + 128 * j, 128), :], sib)
        for j in range(4)
    ]
    c_in = [
        links.send(pq.at[group(own_at + 128 * j + SEG * (1 - c)), :], xb.at[pl.ds(CRECV + 128 * j, 128), :], sib)
        for j in range(4)
    ]
    half = pl.ds(0, HALF)
    AFTER, GATE, N2, DH2 = (HALF * k for k in range(4))
    SR, W, RD, A, V, SN, SD = (lax.rem(mine_at + HALF * k, 2 * R_ROWS) for k in range(1, 8))
    first_in = [
        bring(s.at[half, :], front4.at[pl.ds(HALF * k, HALF), :]) for k, s in enumerate((after_h, gate_h, n2_h, dh2_h))
    ]
    first_in += [bring(adj_h.at[rows(own_at, HALF), :], adj), bring(wg_h, wg), bring(r2_h.at[half, :], r2)]
    first_in += [bring(wo_h, wo)]
    second_in = [
        bring(s.at[half, :], red.at[rows(spot, HALF), :])
        for s, spot in ((a_h, A), (v_h, V), (sr_h, SR), (w_h, W), (rd_h, RD), (sn_h, SN), (sd_h, SD))
    ]
    lanes = pl.ds(pl.multiple_of(c * HALF_D, 128), HALF_D)
    third_in = [
        bring(s.at[half, lanes], d)
        for s, d in (
            (mixed_h, mixed), (chrec_h, chrec), (keyed_h, keyed), (valued_h, valued), (recepted_h, recepted),
        )
    ]
    third_in += [bring(r1_h.at[half, :], r1), bring(wr_h, wr)]
    b_in = []

    def other_half():
        for j in range(4):
            part_in[j].wait()
            a_in[j].wait_recv()
            for at in (128 * j, 128 * j + SEG):
                add_into(xb, PART + at, [(xb, ARECV + at)], SEG)
                b_in.append(links.send(xb.at[pl.ds(PART + at, SEG), :], xb.at[pl.ds(BRECV + at, SEG), :], opp))
                yield

    seg0 = h * (HALF // SEG)
    not_last = (1 - h).astype(F32)

    def fold(v):
        return jnp.sum(v.reshape(-1, 8, D), axis=0)

    def tally(k, v):
        acc[pl.ds(8 * k, 8), :] += fold(v)

    GAIN1, BIAS1, MIXK, MIXV, MIXR, LOGD, REW, GAIN2, BIAS2, CMIXK, CMIXR = range(NVEC)

    def take(j):
        fin_in[j].wait()
        c_in[j].wait_recv()
        b_in[2 * j].wait_recv()
        b_in[2 * j + 1].wait_recv()
        add_into(fin, 2 * (128 * j + SEG * c), [(xb, CRECV + 128 * j), (xb, BRECV + 128 * j)], 128)
        mine = fin.at[group(128 * j + SEG * c), :]
        links.sent(b_in[2 * j])
        links.sent(b_in[2 * j + 1])
        return links.send(mine, mine, sib)

    def gate_part(j):
        lo = 128 * j
        for seg in range(2):
            live = flags[1, seg0 + 2 * j + seg]

            def body(r, seg=seg, live=live):
                at = lo + SEG * seg + r
                gate = front4[rows(GATE + at, SUB), :]
                co = fin[rows(2 * (lo + SEG * seg) + r, SUB), :]
                res = live * (front4[rows(AFTER + at, SUB), :] + gate * co)
                front4[rows(AFTER + at, SUB), :] = res.astype(BF16).astype(F32)
                go = adj[rows(at, SUB), :].astype(F32) * live
                gg[rows(at, SUB), :] = (go * co * gate * (1.0 - gate)).astype(BF16)

            each(SEG // SUB, SUB, body)
        t0[...] = nt(gg[pl.ds(lo, 128), :], wg[...])
        for seg in range(2):

            def body2(r, seg=seg):
                at = 2 * (lo + SEG * seg) + r
                qk = fin[rows(at + SEG, SUB), :]
                qr = t0[rows(SEG * seg + r, SUB), :]
                dh2 = front4[rows(DH2 + lo + SEG * seg + r, SUB), :]
                tally(CMIXK, qk * dh2)
                tally(CMIXR, qr * dh2)
                base = qk * ck[...] + qr * cr[...]
                fin[rows(at, SUB), :] = base
                fin[rows(at + SEG, SUB), :] = (qk + qr) - base

            each(SEG // SUB, SUB, body2)

    def lifted(nxt, u):
        row = lax.broadcasted_iota(jnp.int32, u.shape, 0)
        return jnp.where(row == u.shape[0] - 1, nxt, pltpu.roll(u, u.shape[0] - 1, 0))

    def norm_back(e, n, r, gain):
        f = e * gain
        return r * (f - jnp.mean(f, axis=-1, keepdims=True) - n * jnp.mean(f * n, axis=-1, keepdims=True))

    def keep_next(seg):
        return 1.0 - flags[0, jnp.minimum(seg0 + seg + 1, NSEG - 1)]

    def walk_rows(j, edge_row, sub_body):
        for seg in (1, 0):
            s = 2 * j + seg
            live = flags[1, seg0 + s]
            for k in reversed(range(SEG // SUB)):
                lo = SEG * s + SUB * k
                at = 2 * SEG * s + SUB * k
                if lo + SUB == HALF:
                    nxt = edge_row[0:1, :] * (not_last * keep_next(s))
                elif k == SEG // SUB - 1:
                    nxt = fin[2 * SEG * (s + 1) + SEG : 2 * SEG * (s + 1) + SEG + 1, :] * keep_next(s)
                else:
                    nxt = fin[at + SEG + SUB : at + SEG + SUB + 1, :]
                sub_body(lo, at, live, nxt)

    def after_rows(lo, at, live, nxt):
        e = fin[pl.ds(at, SUB), :] + lifted(nxt, fin[pl.ds(at + SEG, SUB), :])
        n = front4[pl.ds(N2 + lo, SUB), :]
        tally(GAIN2, e * n)
        tally(BIAS2, e)
        go = adj[pl.ds(lo, SUB), :].astype(F32) * live
        ga = go + norm_back(e, n, r2[pl.ds(lo, SUB), 0:1], g2[...])
        front4[pl.ds(N2 + lo, SUB), :] = ga
        gb[pl.ds(lo, SUB), :] = ga.astype(BF16)

    def mixed_chunk(j):
        t0[...] = nt(gb[pl.ds(128 * j, 128), :], wo[...])
        for seg in (1, 0):
            total = 16 * (2 * j + seg)
            sums[pl.ds(total, 16), :] = jnp.zeros((16, D), F32)

            def body(r, seg=seg, total=total):
                at = 128 * j + SEG * seg + r
                gm = t0[rows(SEG * seg + r, SUB), :]
                sr = red[rows(SR + at, SUB), :]
                w = red[rows(W + at, SUB), :]
                gw = gm * sr
                q = gw * red[rows(RD + at, SUB), :]
                red[rows(RD + at, SUB), :] = q
                gp[rows(at, SUB), :] = (gw * w * (1.0 - sr)).astype(BF16)
                fq = fade[rows(r, SUB), :] * q
                sums[pl.ds(total, 8), :] += fold(fq)
                sums[pl.ds(total + 8, 8), :] += fold(fq * w)

            each(SEG // SUB, SUB, body)

    def chain():
        first = jnp.zeros((1, D), F32)
        second = jnp.zeros((1, D), F32)
        th = through[...]
        for s in reversed(range(8)):
            q = jnp.sum(sums[pl.ds(16 * s, 8), :], axis=0, keepdims=True)
            qw = jnp.sum(sums[pl.ds(16 * s + 8, 8), :], axis=0, keepdims=True)
            if s < 7:
                q = q + th * (first * keep_next(s))
                qw = qw + th * (second * keep_next(s))
            first, second = q, qw
        sums[0:1, :] = first
        sums[1:2, :] = second

    tri = triangle(True)

    def key_value(k, carry):
        s = 7 - k
        lo = SEG * s
        keep = 1.0 - flags[0, seg0 + s]
        for col in range(D // 128):
            cols = pl.ds(col * 128, 128)
            at = rows(lo, SEG)
            q = red[rows(RD + lo, SEG), cols]
            w = red[rows(W + lo, SEG), cols]
            a = red[rows(A + lo, SEG), cols]
            v = red[rows(V + lo, SEG), cols]
            fq = fade[:, cols] * q
            cum, both = running(tri, fq, fq * w)
            cn = through[:, cols] * gc[0:1, cols]
            cd = through[:, cols] * gc[1:2, cols]
            gn = rise[:, cols] * (cum[:, :128] + cn)
            gd = rise[:, cols] * (cum[:, 128:] + cd)
            gc[0:1, cols] = (both[0:1, :128] + cum[0:1, :128] + cn) * keep
            gc[1:2, cols] = (both[0:1, 128:] + cum[0:1, 128:] + cd) * keep
            eq = expu[:, cols] * a * q
            gvv = a * gn + eq
            gv[at, cols] = gvv.astype(BF16)
            gk[at, cols] = (v * gvv - (a * gd + eq * w)).astype(BF16)
            up = eq * (v - w)
            down = gn * red[rows(SN + lo, SEG), cols] - gd * red[rows(SD + lo, SEG), cols]
            acc[pl.ds(8 * REW, 8), cols] += jnp.sum(up.reshape(-1, 8, 128), axis=0)
            acc[pl.ds(8 * LOGD, 8), cols] += jnp.sum(down.reshape(-1, 8, 128), axis=0)
        return carry

    def weights(k, left, right):
        for col in range(D // 256):
            cols = pl.ds(256 * col, 256)
            red[rows(mine_at + HALF_D * k, HALF_D), cols] = tn(left[...], right[:, cols])

    shared = []

    def share(ref):
        if not shared:
            pl.semaphore_wait(ready_sib, 1)
        shared.append(links.send(ref, ref, sib))

    orders = ((ax, az, ay), (az, ax, ay), (ax, az, ay), (az, ax, ay), (ay, ax, az))

    def reduce_weights(k):
        if k == 0:
            pl.semaphore_wait(ready_ring, 6)
        first, second, third = orders[k]
        yield from all_reduce(
            links, red, mine_at + HALF_D * k, HALF_D, (first, second), xb, HALF_D * k,
            with_ring(third), yland, HALF_D // 4 * k, red, None, share,
        )

    def front_chunk(j):
        at0 = pl.ds(128 * j, 128)
        t0[...] = nt(gk[at0, :], wk[...])
        t1[...] = nt(gv[at0, :], wv[...])
        t2[...] = nt(gp[at0, :], wr[...])
        for seg in range(2):

            def body(r, seg=seg):
                lo = 128 * j + SEG * seg
                pk, pv_, pr = (t[rows(SEG * seg + r, SUB), :] for t in (t0, t1, t2))
                dh1 = front4[rows(DH2 + lo + r, SUB), :]
                tally(MIXK, pk * dh1)
                tally(MIXV, pv_ * dh1)
                tally(MIXR, pr * dh1)
                base = pk * fk[...] + pv_ * fv[...] + pr * fr[...]
                fin[rows(2 * lo + r, SUB), :] = base
                fin[rows(2 * lo + SEG + r, SUB), :] = (pk + pv_ + pr) - base

            each(SEG // SUB, SUB, body)

    def input_rows(lo, at, live, nxt):
        e = fin[pl.ds(at, SUB), :] + lifted(nxt, fin[pl.ds(at + SEG, SUB), :])
        n = front4[pl.ds(GATE + lo, SUB), :]
        tally(GAIN1, e * n)
        tally(BIAS1, e)
        gi[rows(own_at + lo, SUB), :] = front4[pl.ds(N2 + lo, SUB), :] + norm_back(e, n, r1[pl.ds(lo, SUB), 0:1], g1[...])

    def vector_sums():
        scale = -jnp.exp(dec[...]) * jnp.exp(-jnp.exp(dec[...]))
        vec_o[...] = jnp.zeros_like(vec_o)
        for k in range(NVEC):
            total = jnp.sum(acc[pl.ds(8 * k, 8), :], axis=0, keepdims=True)
            vec_o[k : k + 1, :] = total * scale if k == LOGD else total

    def cast_rows(r):
        out_o[rows(own_at + r, SUB), :] = front4[rows(AFTER + r, SUB), :].astype(BF16)
        out_o[rows(other_at + r, SUB), :] = other[rows(r, SUB), :].astype(BF16)

    wk, wv = wg, wo

    def compute():
        for k, v in enumerate(given):
            pv[k : k + 1, :] = v[...].reshape(1, D)
        through[...] = decay_tables(dec[...], rise, fade)
        expu[...] = jnp.exp(rew[...])
        acc[...] = jnp.zeros_like(acc)
        for copy in first_in:
            copy.wait()
        yield
        for j in range(4):
            e_in = take(j)
            if j == 3:
                for device in (xp, xm, zp, zm, yp, ym):
                    pl.semaphore_signal(ready_ring, inc=1, device_id=device, device_id_type=MESH)
            yield
            e_in.wait_recv()
            links.sent(e_in)
            gate_part(j)
            if j == 0:
                gsend[...] = fin[SEG : SEG + 8, :]
                u_in = links.send(gsend, urow, opp)
            yield
        wk_in = bring(wk_h, wk)
        u_in.wait_recv()
        for copy in second_in:
            copy.wait()
        for j in reversed(range(4)):
            walk_rows(j, urow, after_rows)
            mixed_chunk(j)
            if j > 0:
                yield
        chain()
        g_in = links.send(sums.at[pl.ds(0, 8), :], grecv, opp)
        late = [wk_in, bring(wv_h, wv), bring(n1_h.at[half, :], front4.at[pl.ds(GATE, HALF), :])]
        late.append(bring(dh1_h.at[half, :], front4.at[pl.ds(DH2, HALF), :]))
        yield
        for copy in third_in:
            copy.wait()
        weights(0, mixed, gb)
        yield
        weights(1, chrec, gg)
        yield
        g_in.wait_recv()
        edge = not_last * keep_next(7)
        gc[0:1, :] = grecv[0:1, :] * edge
        gc[1:2, :] = grecv[1:2, :] * edge
        lax.fori_loop(0, 4, key_value, 0)
        yield
        lax.fori_loop(4, 8, key_value, 0)
        pl.semaphore_signal(ready_sib, inc=1, device_id=sib, device_id_type=MESH)
        yield
        weights(2, recepted, gp)
        yield
        weights(3, keyed, gk)
        yield
        weights(4, valued, gv)
        yield
        for copy in late:
            copy.wait()
        for j in range(4):
            front_chunk(j)
            if j == 0:
                u2_in = links.send(fin.at[pl.ds(SEG, 8), :], urow2, opp)
            yield
        u2_in.wait_recv()
        for j in reversed(range(4)):
            walk_rows(j, urow2, input_rows)
            if j == 2:
                yield
        vector_sums()

    def vectors():
        for k, (place, others) in enumerate(((x, (xp, xo, xm)), (z, (zp, zo, zm)), (y, (yp, opp, ym)))):
            yield from sum_of_four(links, vec_o, 0, 16, place, others, vland, 64 * k)

    def swap(src, src_at, dst, dst_at, back_at):
        there = []
        for k in range(4):
            there.append(
                links.send(src.at[rows(src_at + SEG * k, SEG), :], dst.at[rows(dst_at + SEG * k, SEG), :], opp)
            )
            yield
        onward = []
        for k in range(4):
            there[k].wait_recv()
            theirs = dst.at[rows(back_at + SEG * k, SEG), :]
            onward.append(links.send(theirs, theirs, sib))
            yield
        for copy in onward:
            copy.wait_recv()

    def result():
        yield from swap(front4, AFTER + 256 * c, other, 256 * c, 256 * c)
        each(HALF // SUB, SUB, cast_rows)

    def input_grads():
        yield from swap(gi, own_at + 256 * c, gi, own_at + 256 * c, other_at + 256 * c)

    jobs = dict(zip("abcd", ffs))
    jobs.update(zip("pqrst", (reduce_weights(k) for k in range(MATS))))
    jobs.update(M=compute(), B=other_half(), V=vectors(), O=result(), G=input_grads())
    for name in "".join(ORDER):
        next(jobs[name], None)
        links.settle(SETTLE)
    for copy in shared:
        copy.wait_recv()
    links.finish()


def back(front_outs, adj, vecs, mats):
    g1, b1, fk, fv, fr, dec, rew, g2, b2, ck, cr = vecs
    flags, rest = front_outs[0], front_outs[1:]
    vm = pltpu.VMEM
    anywhere = pl.BlockSpec(memory_space=pl.ANY)
    vmem = pl.BlockSpec(memory_space=pltpu.VMEM)
    half = lambda dt: vm((HALF, D), dt)
    return pl.pallas_call(
        back_kernel,
        in_specs=[pl.BlockSpec(memory_space=pltpu.SMEM)] + [anywhere] * len(rest) + [anywhere]
        + [vmem] * 9 + [anywhere] * 5,
        out_specs=[vmem] * 5,
        out_shape=[vm((T, D), BF16), vm((T, D), F32), vm((16, D), F32), vm((2 * R_ROWS, D), F32), vm((FF_ROWS, D), F32)],
        scratch_shapes=[vm((4 * HALF, D), F32), vm((HALF, 128), F32), vm((HALF, 128), F32)]
        + [vm((HALF, HALF_D), BF16)] * 5 + [half(BF16)] + [vm((D, D), BF16)] * 3
        + [vm((2 * HALF, D), F32), vm((R_ROWS, D), F32)]
        + [half(BF16)] * 5 + [vm((128, D), F32)] * 3 + [half(F32)]
        + [vm((FF_ROWS, D), F32), vm((R_ROWS // 4, D), F32), vm((192, D), F32)]
        + [vm((8, D), F32)] * 4 + [vm((8 * NVEC, D), F32)] + [vm((SEG, D), F32)] * 2
        + [vm((1, D), F32)] * 2 + [vm((128, D), F32), vm((8, D), F32), vm((16, D), F32)]
        + [pltpu.SemaphoreType.DMA((COPIES,)), pltpu.SemaphoreType.DMA((COPIES,)),
           pltpu.SemaphoreType.DMA((48,)), pltpu.SemaphoreType.REGULAR, pltpu.SemaphoreType.REGULAR],
        compiler_params=pltpu.CompilerParams(collective_id=1, has_side_effects=True, vmem_limit_bytes=BACK_VMEM * 2**20),
        cost_estimate=pl.CostEstimate(flops=14 * T * D * D, bytes_accessed=60 * 2**20, transcendentals=0),
        name="back",
    )(flags, *rest, adj, g1, fk, fv, fr, dec, rew, g2, ck, cr, *mats[:5])


def finish_kernel(out, gi, vec, red, ff, *refs):
    out_o, gi_o, mats, ck_o, cv_o, vecs, sems = refs[0], refs[1], refs[2:7], refs[7], refs[8], refs[9:20], refs[20]
    pairs = [(gi, gi_o), (ff.at[pl.ds(0, D), :], ck_o), (ff.at[pl.ds(D, D), :], cv_o), (out, out_o)]
    for k in range(MATS):
        for core in range(2):
            src = red.at[pl.ds(core * R_ROWS + HALF_D * k, HALF_D), :]
            pairs.append((src, mats[(3, 4, 0, 1, 2)[k]].at[pl.ds(HALF_D * core, HALF_D), :]))
    copies = [pltpu.make_async_copy(src, dst, sems.at[k]) for k, (src, dst) in enumerate(pairs)]
    for copy in copies:
        copy.start()
    for k in range(NVEC):
        vecs[k][...] = vec[k : k + 1, :].reshape(D)
    for copy in copies:
        copy.wait()


def finish(out, gi, vec, red, ff):
    sds = jax.ShapeDtypeStruct
    anywhere = pl.BlockSpec(memory_space=pl.ANY)
    vmem = pl.BlockSpec(memory_space=pltpu.VMEM)
    return pl.pallas_call(
        finish_kernel,
        in_specs=[vmem] * 5,
        out_specs=[anywhere] * 9 + [vmem] * NVEC,
        out_shape=[sds((T, D), BF16), sds((T, D), F32)] + [sds((D, D), F32)] * 7 + [sds((D,), F32)] * NVEC,
        scratch_shapes=[pltpu.SemaphoreType.DMA((16,))],
        compiler_params=pltpu.CompilerParams(vmem_limit_bytes=FINISH_VMEM * 2**20),
        name="finish",
    )(out, gi, vec, red, ff)


def body(
    entering_activations, sample_sizes, initial_layernorm_scale, initial_layernorm_offset, temporal_lookup_fraction,
    temporal_content_fraction, temporal_gating_fraction, fading_speed_logarithm, present_reward,
    temporal_gating_matrix, temporal_lookup_matrix, temporal_content_matrix, temporal_emission_matrix,
    latter_layernorm_scale, latter_layernorm_offset, feedforward_lookup_fraction, feedforward_gating_fraction,
    feedforward_gating_matrix, feedforward_lookup_matrix, feedforward_content_matrix, upstream_adjoint,
):
    vecs = (
        initial_layernorm_scale, initial_layernorm_offset, temporal_lookup_fraction, temporal_content_fraction,
        temporal_gating_fraction, fading_speed_logarithm, present_reward, latter_layernorm_scale,
        latter_layernorm_offset, feedforward_lookup_fraction, feedforward_gating_fraction,
    )
    mats = (
        temporal_gating_matrix, temporal_lookup_matrix, temporal_content_matrix, temporal_emission_matrix,
        feedforward_gating_matrix, feedforward_lookup_matrix, feedforward_content_matrix,
    )
    half = (lax.axis_index("tensor") // 2).astype(jnp.int32).reshape(1)
    fronts = front(half, sample_sizes, entering_activations, upstream_adjoint, vecs, mats)
    out, grad_inputs, recw, keyw, valw, outw, chrec, chkey, chval, *g = finish(*back(fronts, upstream_adjoint, vecs, mats))
    return (
        out, grad_inputs, g[0], g[1], g[2], g[3], g[4], g[5], g[6], recw, keyw, valw, outw,
        g[7], g[8], g[9], g[10], chrec, chkey, chval,
    )


def solution(mesh):
    split = P("dp", None)
    in_specs = (split, split) + (P(),) * 16 + (P(None, "tensor"), P("tensor", None), split)
    out_specs = (split, split) + (P(),) * 16 + (P(None, "tensor"), P("tensor", None))
    return jax.shard_map(body, mesh=mesh, in_specs=in_specs, out_specs=out_specs, check_vma=False)
```

profile of v0, /device:TPU:1, one launch (start us, length us, event | category | flops | bytes accessed | tf_op | source)
XLA Modules:
  0.0 174.6 jit_solution(1690296862042391764)
XLA Ops:
  0.7 28.1 %front.1 = (f32[2,16]{1,0:T(2,128)}, f32[2048,768]{1,0:T(8,128)}, f32[1536,768]{1,0:T(8,128)}, f32[512,768]{1,0:T(8,128)}, f32[512,768]{1,0:T(8,128)}, /*index=5...) custom-call(s32[1]{0:T(128)} %bitcast.half_ref, ...), custom_call_target="tpu_custom_call" | custom-call | flops 13287555072 | bytes 62914560 | tf_op jit(solution)/shard_map/front/pallas_call | solution.py:296
  28.8 137.7 %back.1 = (bf16[1024,768]{1,0:T(8,128)(2,1)S(1)}, f32[1024,768]{1,0:T(8,128)S(1)}, f32[16,768]{1,0:T(8,128)S(1)}, f32[4096,768]{1,0:T(8,128)S(1)}, f32[1536,768]{1,0:T(8,128)S(1)}) custom-call(f32[2,16]{1,0:T(2,128)} %get-tuple-element.68.flags, f32[2048,768]{1,0:T(8,128)} %get-tuple-element.69.pq, f32[1536,768]{1,0:T(8,128)} %get-tuple-element.70.grads, ...), custom_call_target="tpu_custom_call" | custom-call | flops 8455716864 | bytes 62914560 | tf_op jit(solution)/shard_map/back/pallas_call | solution.py:968
  166.5 8.0 %finish.1 = (bf16[1024,768]{1,0:T(8,128)(2,1)}, f32[1024,768]{1,0:T(8,128)}, f32[768,768]{1,0:T(8,128)}, f32[768,768]{1,0:T(8,128)}, f32[768,768]{1,0:T(8,128)},...) custom-call(bf16[1024,768]{1,0:T(8,128)(2,1)S(1)} %get-tuple-element, ...), custom_call_target="tpu_custom_call" | custom-call | tf_op jit(solution)/shard_map/finish/pallas_call | solution.py:1009
where the time goes:
time: 175 us
  Pallas kernels  174 us (99%)
    pallas_call x1, Pallas kernels, back(): pl.pallas_call(back_kernel, in_specs=[pl.BlockSpec(memory_space=pltpu.SME...  138 us
    pallas_call x1, Pallas kernels, front(): pl.pallas_call(front_kernel, grid_spec=pltpu.PrefetchScalarGridSpec(num_s...  28.1 us
    pallas_call x1, Pallas kernels, finish(): pl.pallas_call(finish_kernel, in_specs=[vmem] * 5, out_specs=[anywhere] *...  7.97 us

commit v1 on v0

--- a/solution.py
+++ b/solution.py
@@ -72,9 +72,21 @@
     return jnp.exp(-float(SEG) * rate)
 
 
-def spread(dst, first, v):
+def spread(dst, first, cols, v):
     for s in range(v.shape[0] // SEG):
-        dst[2 * SEG * s + first : 2 * SEG * s + first + SEG, :] = v[SEG * s : SEG * (s + 1), :]
+        dst[first + 2 * SEG * s : first + 2 * SEG * s + SEG, cols] = v[SEG * s : SEG * (s + 1), :]
+
+
+def weave(products, others):
+    done = 0
+    for k, product in enumerate(products):
+        product()
+        upto = len(others) * (k + 1) // len(products)
+        for other in others[done:upto]:
+            other()
+        done = upto
+    for other in others[done:]:
+        other()
 
 
 def front_kernel(
@@ -83,10 +95,11 @@
     flags, pq, grads, n1_h, dh1_h, a_h, v_h, sr_h, w_h, rd_h, sn_h, sd_h, after_h, gate_h, n2_h, dh2_h,
     r1_h, r2_h, keyed_h, valued_h, recepted_h, mixed_h, chrec_h,
     wr, wk, wv, wo, wg, wfk, wfv, wide, narrow, low, gbuf,
-    rise, fade, through, expu, nc, dc, p1, p2, kb, vb, rb, hb, cks, hid, gch, gpr, pv, win, outs, gsem,
+    rise, fade, through, expu, nc, dc, p1, p2, kb, vb, rb, hb, cks_all, hid_all, gch_all, gpr_all, pv, win, outs, gsem,
 ):
     i = pl.program_id(0)
-    slot = lax.rem(i, SLOTS)
+    slot = lax.rem(i, SLOTS) if SLOTS > 1 else 0
+    cks, hid, gch, gpr = (ref.at[i] for ref in (cks_all, hid_all, gch_all, gpr_all))
     given = (g1_h, b1_h, fk_h, fv_h, fr_h, dec_h, rew_h, g2_h, b2_h, ck_h, cr_h)
     g1, b1, fk, fv, fr, dec, rew, g2, b2, ck, cr = (pv.at[k : k + 1, :] for k in range(len(given)))
     n1_o, dh1_o, a_o, v_o, sr_o, w_o, rd_o, sn_o, sd_o, after_o, gate_o, n2_o, dh2_o = (
@@ -167,7 +180,13 @@
     fresh = [flags[0, i * (BLK // SEG) + s] for s in range(BLK // SEG)]
     live = [flags[1, i * (BLK // SEG) + s] for s in range(BLK // SEG)]
 
-    for s in range(BLK // SUB):
+    tri = triangle(False)
+    part = BLK // 2
+    subs = part // SUB
+    segs = part // SEG
+    col_tiles = [pl.ds(0, D)]
+
+    def first_norm(s):
         at = pl.ds(s * SUB, SUB)
         n1, r1 = normalize(x_ref[at, :].astype(F32))
         h1 = n1 * g1[...] + b1[...]
@@ -184,51 +203,35 @@
         dh1_o[at, :] = dh1
         r1_o[at, :] = jnp.broadcast_to(r1, (SUB, 128))
 
-    save(0, 6)
-    reuse(6, 14)
-    loaded(0, 3)
-    kb[...] = nn(keyed_o[...], wk[...])
-    vb[...] = nn(valued_o[...], wv[...])
-    rb[...] = nn(recepted_o[...], wr[...])
-
-    tri = triangle(False)
-    for s in range(BLK // SEG):
+    def mix_time(s, c):
         at = pl.ds(s * SEG, SEG)
         keep = 1.0 - fresh[s]
-        for c in range(D // 128):
-            cols = pl.ds(c * 128, 128)
-            a = jnp.exp(kb[at, cols])
-            v = vb[at, cols]
-            lift = rise[:, cols] * a
-            cum, both = running(tri, lift * v, lift)
-            ncar = nc[:, cols] * keep
-            dcar = dc[:, cols] * keep
-            sn = fade[:, cols] * (ncar + cum[:, :128])
-            sd = fade[:, cols] * (dcar + cum[:, 128:])
-            th = through[:, cols]
-            nc[:, cols] = th * (ncar + (cum[SEG - 1 :, :128] + both[SEG - 1 :, :128]))
-            dc[:, cols] = th * (dcar + (cum[SEG - 1 :, 128:] + both[SEG - 1 :, 128:]))
-            e = expu[:, cols] * a
-            rd = 1.0 / (sd + e)
-            w = (sn + e * v) * rd
-            sr = jax.nn.sigmoid(rb[at, cols])
-            mixed_o[at, cols] = (sr * w).astype(BF16)
-
-            a_o[at, cols] = a
-            v_o[at, cols] = v
-            sr_o[at, cols] = sr
-            w_o[at, cols] = w
-            rd_o[at, cols] = rd
-            sn_o[at, cols] = sn
-            sd_o[at, cols] = sd
-
-    save(6, 14)
-    reuse(14, 20)
-    loaded(3, 4)
-    hb[...] = nn(mixed_o[...], wo[...])
-
-    rows0 = pl.multiple_of(i * BLK, BLK)
-    for s in range(BLK // SUB):
+        cols = pl.ds(c * 128, 128)
+        a = jnp.exp(kb[at, cols])
+        v = vb[at, cols]
+        lift = rise[:, cols] * a
+        cum, both = running(tri, lift * v, lift)
+        ncar = nc[:, cols] * keep
+        dcar = dc[:, cols] * keep
+        sn = fade[:, cols] * (ncar + cum[:, :128])
+        sd = fade[:, cols] * (dcar + cum[:, 128:])
+        th = through[:, cols]
+        nc[:, cols] = th * (ncar + (cum[SEG - 1 :, :128] + both[SEG - 1 :, :128]))
+        dc[:, cols] = th * (dcar + (cum[SEG - 1 :, 128:] + both[SEG - 1 :, 128:]))
+        e = expu[:, cols] * a
+        rd = 1.0 / (sd + e)
+        w = (sn + e * v) * rd
+        sr = jax.nn.sigmoid(rb[at, cols])
+        mixed_o[at, cols] = (sr * w).astype(BF16)
+        a_o[at, cols] = a
+        v_o[at, cols] = v
+        sr_o[at, cols] = sr
+        w_o[at, cols] = w
+        rd_o[at, cols] = rd
+        sn_o[at, cols] = sn
+        sd_o[at, cols] = sd
+
+    def second_norm(s):
         at = pl.ds(s * SUB, SUB)
         after = x_ref[at, :].astype(F32) + hb[at, :]
         n2, r2 = normalize(after)
@@ -239,41 +242,94 @@
         sh = roll_down(h2, before)
         p2[...] = h2[SUB - 1 :, :]
         dh2 = h2 - sh
-        cks[pl.ds(rows0 + s * SUB, SUB), :] = (sh + dh2 * ck[...]).astype(BF16)
+        cks[at, :] = (sh + dh2 * ck[...]).astype(BF16)
         chrec_o[at, :] = (sh + dh2 * cr[...]).astype(BF16)
         after_o[at, :] = after
         n2_o[at, :] = n2
         dh2_o[at, :] = dh2
         r2_o[at, :] = jnp.broadcast_to(r2, (SUB, 128))
 
-    save(14, 19)
-    loaded(4, 7)
-    rows = pl.ds(rows0, BLK)
-    hb[...] = nn(cks[rows, :], wfk[...])
-    gate_o[...] = nn(chrec_o[...], wg[...])
-    for s in range(BLK // SUB):
+    def gates(s):
         at = pl.ds(s * SUB, SUB)
-        hp = jnp.maximum(hb[at, :], 0.0)
-        hid[pl.ds(rows0 + s * SUB, SUB), :] = (hp * hp).astype(BF16)
-        gate = jax.nn.sigmoid(gate_o[at, :])
+        hp = jnp.maximum(kb[at, :], 0.0)
+        hid[at, :] = (hp * hp).astype(BF16)
+        gate = jax.nn.sigmoid(rb[at, :])
         gate_o[at, :] = gate
         go = adj_ref[at, :].astype(F32) * live[s * SUB // SEG]
-        gch[pl.ds(rows0 + s * SUB, SUB), :] = (go * gate).astype(BF16)
+        gch[at, :] = (go * gate).astype(BF16)
+
+    def hidden_grads(s):
+        at = pl.ds(s * SUB, SUB)
+        gpr[at, :] = (2.0 * jnp.maximum(kb[at, :], 0.0) * vb[at, :]).astype(BF16)
+
+    def all_of(fn, p, count):
+        return [functools.partial(fn, p * count + k) for k in range(count)]
+
+    def times(p, dst, left, right):
+        at = pl.ds(p * part, part)
+
+        def piece(cols):
+            dst[at, cols] = nn(left[at, :], right[:, cols])
+
+        return [functools.partial(piece, cols) for cols in col_tiles]
+
+    def times_turned(p, dst, left, right):
+        at = pl.ds(p * part, part)
+
+        def piece(cols):
+            dst[at, cols] = nt(left[at, :], right[cols, :])
+
+        return [functools.partial(piece, cols) for cols in col_tiles]
+
+    def to_pq(p, first, product, left, right):
+        at = pl.ds(p * part, part)
+
+        def piece(cols):
+            v = nn(left[at, :], right[:, cols]) if product is nn else nt(left[at, :], right[cols, :])
+            spread(pq, 2 * p * part + first, cols, v)
+
+        return [functools.partial(piece, cols) for cols in col_tiles]
+
+    def projections(p):
+        return times(p, kb, keyed_o, wk) + times(p, vb, valued_o, wv) + times(p, rb, recepted_o, wr)
+
+    def mixing(p):
+        return [functools.partial(mix_time, p * segs + s, c) for s in range(segs) for c in range(D // 128)]
+
+    def hidden(p):
+        return times(p, kb, cks, wfk) + times(p, rb, chrec_o, wg)
+
+    def outward(p):
+        return to_pq(p, 0, nn, hid, wfv) + times_turned(p, vb, gch, wfv)
+
+    weave([], all_of(first_norm, 0, subs))
+    loaded(0, 3)
+    weave(projections(0), all_of(first_norm, 1, subs))
+    save(0, 6)
+    reuse(6, 14)
+    loaded(3, 4)
+    weave(projections(1), mixing(0))
+    weave(times(0, hb, mixed_o, wo), mixing(1))
+    save(6, 14)
+    reuse(14, 20)
+    loaded(4, 7)
+    weave(times(1, hb, mixed_o, wo), all_of(second_norm, 0, subs))
+    weave(hidden(0), all_of(second_norm, 1, subs))
+    save(14, 19)
+    weave(hidden(1), all_of(gates, 0, subs))
+    weave(outward(0), all_of(gates, 1, subs))
     save(19, 20)
-    spread(pq, 0, nn(hid[rows, :], wfv[...]))
-    kb[...] = nt(gch[rows, :], wfv[...])
-    for s in range(BLK // SUB):
-        at = pl.ds(s * SUB, SUB)
-        gpr[pl.ds(rows0 + s * SUB, SUB), :] = (2.0 * jnp.maximum(hb[at, :], 0.0) * kb[at, :]).astype(BF16)
-    spread(pq, SEG, nt(gpr[rows, :], wfk[...]))
+    weave(outward(1), all_of(hidden_grads, 0, subs))
+    weave(to_pq(0, SEG, nt, gpr, wfk), all_of(hidden_grads, 1, subs))
+    weave(to_pq(1, SEG, nt, gpr, wfk), [])
 
     @pl.when(i == T // BLK - 1)
     def _():
         out_copies = []
-        for k, (left, right) in enumerate(((cks, gpr), (hid, gch))):
+        for k, (left, right) in enumerate(((cks_all, gpr_all), (hid_all, gch_all))):
             for c in range(D // 256):
                 at = pl.ds(D * k + 256 * c, 256)
-                gbuf[at, :] = tn(left[:, pl.ds(256 * c, 256)], right[...])
+                gbuf[at, :] = tn(left[:, :, pl.ds(256 * c, 256)].reshape(T, 256), right[...].reshape(T, D))
                 out_copies.append(pltpu.make_async_copy(gbuf.at[at, :], grads.at[at, :], gsem.at[3 * k + c]))
                 out_copies[-1].start()
         for copy in out_copies:
@@ -304,7 +360,7 @@
             scratch_shapes=[vm((D, D), BF16)] * 7
             + [vm((SLOTS, 13, BLK, D), F32), vm((SLOTS, 2, BLK, 128), F32), vm((SLOTS, 5, BLK, D), BF16), vm((2 * D, D), F32)]
             + [vm((SEG, D), F32)] * 2 + [vm((1, D), F32)] * 6 + [vm((BLK, D), F32)] * 4
-            + [vm((T, D), BF16)] * 4 + [vm((16, D), F32)]
+            + [vm((T // BLK, BLK, D), BF16)] * 4 + [vm((16, D), F32)]
             + [pltpu.SemaphoreType.DMA((7,)), pltpu.SemaphoreType.DMA((SLOTS, 20)), pltpu.SemaphoreType.DMA((6,))],
         ),
         out_shape=[sds((2, NSEG), F32), sds((2 * T, D), F32), sds((2 * D, D), F32)]
@@ -323,10 +379,11 @@
 BACK_VMEM = 39
 FINISH_VMEM = 2
 SETTLE = 24
+NEAR = (0, 1, 2, 3, 4)
 ORDER = (
-    "cbBaBMdbBBaBcdBMabdcabdcBabBdMMcMaMbMMdcMOMMbMMO",
-    "OcMMpqMMMMMsMtpqrOMOMMMtpsrqMGptrsdaOOqrtsVpqdtV",
-    "OrGsqGcptGGasrpbqtrsGVpGqtOsGrGV",
+    "bcBBBMbBcBadbcMaMcdbMBBcbaMdMMBcbMaMMbdcMMMMpMOq",
+    "MMOMMrsMtpsrOdcqtMsOaMMprqMtaOdsMqMpstrqdtGVbGpr",
+    "psGrtOOqVpsGOtqdraGGVGsptGrOqGVa",
 )
 NVEC = 11
 
@@ -492,14 +549,21 @@
     each(size // 8, 8, body)
 
 
-def all_reduce(links, data, base, size, axes, land, land_at, last, last_land, last_at, source, loaded, share):
-    (place, up, _, down), (place_2, *others) = axes
+def all_reduce(links, data, base, size, axes, land, land_at, last, last_land, last_at, source, loaded, share, near):
+    (place, up, _, down), (place_2, up_2, opp_2, down_2) = axes
+    others = (up_2, opp_2, down_2)
     yield from ring_reduce(links, data, base, size, place, up, down, land, land_at, source, loaded)
     part = size // 4
     at = base + place * part
-    yield from near_reduce(links, data, at, part, place_2, others, land, land_at + 3 * part, land_at + part)
+    if near:
+        yield from near_reduce(links, data, at, part, place_2, others, land, land_at + 3 * part, land_at + part)
+    else:
+        yield from ring_reduce(links, data, at, part, place_2, up_2, down_2, land, land_at + 3 * part, data, None)
     yield from last(links, data, at + place_2 * (part // 4), part // 4, last_land, last_at)
-    yield from near_gather(links, data, at, part, place_2, others)
+    if near:
+        yield from near_gather(links, data, at, part, place_2, others)
+    else:
+        yield from ring_gather(links, data, at, part, place_2, up_2, down_2, lambda ref: None)
     yield from ring_gather(links, data, base, size, place, up, down, share)
 
 
@@ -587,7 +651,7 @@
     ffs = [
         all_reduce(
             links, ff, n * k, n, (ax, az) if k % 2 == 0 else (az, ax), ffland, n * k,
-            with_pair, ffland, n * k + 15 * n // 16, grads, ff_loaded, lambda ref: None,
+            with_pair, ffland, n * k + 15 * n // 16, grads, ff_loaded, lambda ref: None, True,
         )
         for k in range(4)
     ]
@@ -620,15 +684,15 @@
         )
     ]
     third_in += [bring(r1_h.at[half, :], r1), bring(wr_h, wr)]
-    b_in = []
+    b_in = {}
 
     def other_half():
-        for j in range(4):
+        for j in (0, 3, 2, 1):
             part_in[j].wait()
             a_in[j].wait_recv()
             for at in (128 * j, 128 * j + SEG):
                 add_into(xb, PART + at, [(xb, ARECV + at)], SEG)
-                b_in.append(links.send(xb.at[pl.ds(PART + at, SEG), :], xb.at[pl.ds(BRECV + at, SEG), :], opp))
+                b_in[at] = links.send(xb.at[pl.ds(PART + at, SEG), :], xb.at[pl.ds(BRECV + at, SEG), :], opp)
                 yield
 
     seg0 = h * (HALF // SEG)
@@ -645,12 +709,12 @@
     def take(j):
         fin_in[j].wait()
         c_in[j].wait_recv()
-        b_in[2 * j].wait_recv()
-        b_in[2 * j + 1].wait_recv()
+        b_in[128 * j].wait_recv()
+        b_in[128 * j + SEG].wait_recv()
         add_into(fin, 2 * (128 * j + SEG * c), [(xb, CRECV + 128 * j), (xb, BRECV + 128 * j)], 128)
         mine = fin.at[group(128 * j + SEG * c), :]
-        links.sent(b_in[2 * j])
-        links.sent(b_in[2 * j + 1])
+        links.sent(b_in[128 * j])
+        links.sent(b_in[128 * j + SEG])
         return links.send(mine, mine, sib)
 
     def gate_part(j):
@@ -806,7 +870,7 @@
         first, second, third = orders[k]
         yield from all_reduce(
             links, red, mine_at + HALF_D * k, HALF_D, (first, second), xb, HALF_D * k,
-            with_ring(third), yland, HALF_D // 4 * k, red, None, share,
+            with_ring(third), yland, HALF_D // 4 * k, red, None, share, k in NEAR,
         )
 
     def front_chunk(j):
@@ -858,9 +922,9 @@
         for copy in first_in:
             copy.wait()
         yield
-        for j in range(4):
+        for j in (0, 3, 2, 1):
             e_in = take(j)
-            if j == 3:
+            if j == 1:
                 for device in (xp, xm, zp, zm, yp, ym):
                     pl.semaphore_signal(ready_ring, inc=1, device_id=device, device_id_type=MESH)
             yield
@@ -871,15 +935,19 @@
                 gsend[...] = fin[SEG : SEG + 8, :]
                 u_in = links.send(gsend, urow, opp)
             yield
-        wk_in = bring(wk_h, wk)
-        u_in.wait_recv()
-        for copy in second_in:
-            copy.wait()
-        for j in reversed(range(4)):
+            if j == 0:
+                continue
+            if j == 3:
+                u_in.wait_recv()
+                for copy in second_in:
+                    copy.wait()
+            if j == 1:
+                wk_in = bring(wk_h, wk)
             walk_rows(j, urow, after_rows)
             mixed_chunk(j)
-            if j > 0:
-                yield
+            yield
+        walk_rows(0, urow, after_rows)
+        mixed_chunk(0)
         chain()
         g_in = links.send(sums.at[pl.ds(0, 8), :], grecv, opp)
         late = [wk_in, bring(wv_h, wv), bring(n1_h.at[half, :], front4.at[pl.ds(GATE, HALF), :])]

time: 175 us -> 173 us (0.989)
  Pallas kernels: 174 us -> 172 us
    pallas_call x1, Pallas kernels: 28.1 us -> 25.6 us  [front(): pl.pallas_call(front_kernel, grid_spec=pltpu.PrefetchScalarGridSpec(num_s...]
where the time goes in v1:
time: 173 us
  Pallas kernels  172 us (99%)
    pallas_call x1, Pallas kernels, back(): pl.pallas_call(back_kernel, in_specs=[pl.BlockSpec(memory_space=pltpu.SME...  138 us
    pallas_call x1, Pallas kernels, front(): pl.pallas_call(front_kernel, grid_spec=pltpu.PrefetchScalarGridSpec(num_s...  25.6 us
    pallas_call x1, Pallas kernels, finish(): pl.pallas_call(finish_kernel, in_specs=[vmem] * 5, out_specs=[anywhere] *...  7.97 us

profile of v1, /device:TPU:1, one launch (start us, length us, event | category | flops | bytes accessed | tf_op | source)
XLA Modules:
  0.0 172.6 jit_solution(4505987517782019615)
XLA Ops:
  0.7 25.6 %front.1 = (f32[2,16]{1,0:T(2,128)}, f32[2048,768]{1,0:T(8,128)}, f32[1536,768]{1,0:T(8,128)}, f32[512,768]{1,0:T(8,128)}, f32[512,768]{1,0:T(8,128)}, /*index=5...) custom-call(s32[1]{0:T(128)} %bitcast.half_ref, ...), custom_call_target="tpu_custom_call" | custom-call | flops 13287555072 | bytes 62914560 | tf_op jit(solution)/shard_map/front/pallas_call | solution.py:352
  26.3 138.2 %back.1 = (bf16[1024,768]{1,0:T(8,128)(2,1)S(1)}, f32[1024,768]{1,0:T(8,128)S(1)}, f32[16,768]{1,0:T(8,128)S(1)}, f32[4096,768]{1,0:T(8,128)S(1)}, f32[1536,768]{1,0:T(8,128)S(1)}) custom-call(f32[2,16]{1,0:T(2,128)} %get-tuple-element.68.flags, f32[2048,768]{1,0:T(8,128)} %get-tuple-element.69.pq, f32[1536,768]{1,0:T(8,128)} %get-tuple-element.70.grads, ...), custom_call_target="tpu_custom_call" | custom-call | flops 8455716864 | bytes 62914560 | tf_op jit(solution)/shard_map/back/pallas_call | solution.py:1036
  164.5 8.0 %finish.1 = (bf16[1024,768]{1,0:T(8,128)(2,1)}, f32[1024,768]{1,0:T(8,128)}, f32[768,768]{1,0:T(8,128)}, f32[768,768]{1,0:T(8,128)}, f32[768,768]{1,0:T(8,128)},...) custom-call(bf16[1024,768]{1,0:T(8,128)(2,1)S(1)} %get-tuple-element, ...), custom_call_target="tpu_custom_call" | custom-call | tf_op jit(solution)/shard_map/finish/pallas_call | solution.py:1077

commit v2 on v1

--- a/solution.py
+++ b/solution.py
@@ -378,12 +378,12 @@
 MATS = 5
 BACK_VMEM = 39
 FINISH_VMEM = 2
-SETTLE = 24
+SETTLE = 14
 NEAR = (0, 1, 2, 3, 4)
 ORDER = (
-    "bcBBBMbBcBadbcMaMcdbMBBcbaMdMMBcbMaMMbdcMMMMpMOq",
-    "MMOMMrsMtpsrOdcqtMsOaMMprqMtaOdsMqMpstrqdtGVbGpr",
-    "psGrtOOqVpsGOtqdraGGVGsptGrOqGVa",
+    "daBBacBdaBBdMMbaMMcdBbMdBBacbMdMaMbMcMbcaMMMOMpM",
+    "qMOMMMrMtsMpMqsObMOrMtqpscrqbsOdMtapqOrsMcOtGOpG",
+    "rtVsGrptOqVGrsGGdqGctVbpGtGrspqV",
 )
 NVEC = 11
 
@@ -618,9 +618,6 @@
         bring(pq.at[group(other_at + 128 * j + SEG * c), :], xb.at[pl.ds(PART + 128 * j, 128), :]) for j in range(4)
     ]
     ff_in = bring(grads, ff)
-    fin_in = [
-        bring(pq.at[group(own_at + 128 * j + SEG * c), :], fin.at[group(128 * j + SEG * c), :]) for j in range(4)
-    ]
     pl.semaphore_wait(barrier, len(partners))
 
     links = Links(sends, recvs)
@@ -660,31 +657,13 @@
         links.send(pq.at[group(other_at + 128 * j + SEG * (1 - c)), :], xb.at[pl.ds(ARECV + 128 * j, 128), :], sib)
         for j in range(4)
     ]
-    c_in = [
-        links.send(pq.at[group(own_at + 128 * j + SEG * (1 - c)), :], xb.at[pl.ds(CRECV + 128 * j, 128), :], sib)
-        for j in range(4)
-    ]
-    half = pl.ds(0, HALF)
     AFTER, GATE, N2, DH2 = (HALF * k for k in range(4))
     SR, W, RD, A, V, SN, SD = (lax.rem(mine_at + HALF * k, 2 * R_ROWS) for k in range(1, 8))
-    first_in = [
-        bring(s.at[half, :], front4.at[pl.ds(HALF * k, HALF), :]) for k, s in enumerate((after_h, gate_h, n2_h, dh2_h))
-    ]
-    first_in += [bring(adj_h.at[rows(own_at, HALF), :], adj), bring(wg_h, wg), bring(r2_h.at[half, :], r2)]
-    first_in += [bring(wo_h, wo)]
-    second_in = [
-        bring(s.at[half, :], red.at[rows(spot, HALF), :])
-        for s, spot in ((a_h, A), (v_h, V), (sr_h, SR), (w_h, W), (rd_h, RD), (sn_h, SN), (sd_h, SD))
-    ]
     lanes = pl.ds(pl.multiple_of(c * HALF_D, 128), HALF_D)
-    third_in = [
-        bring(s.at[half, lanes], d)
-        for s, d in (
-            (mixed_h, mixed), (chrec_h, chrec), (keyed_h, keyed), (valued_h, valued), (recepted_h, recepted),
-        )
-    ]
-    third_in += [bring(r1_h.at[half, :], r1), bring(wr_h, wr)]
+    half = pl.ds(0, HALF)
     b_in = {}
+    c_in = []
+    fin_in = []
 
     def other_half():
         for j in (0, 3, 2, 1):
@@ -860,7 +839,7 @@
     def share(ref):
         if not shared:
             pl.semaphore_wait(ready_sib, 1)
-        shared.append(links.send(ref, ref, sib))
+        shared.append((links.step, links.send(ref, ref, sib)))
 
     orders = ((ax, az, ay), (az, ax, ay), (ax, az, ay), (az, ax, ay), (ay, ax, az))
 
@@ -914,13 +893,34 @@
     wk, wv = wg, wo
 
     def compute():
+        fin_in.extend(
+            bring(pq.at[group(own_at + 128 * j + SEG * c), :], fin.at[group(128 * j + SEG * c), :]) for j in range(4)
+        )
+        c_in.extend(
+            links.send(pq.at[group(own_at + 128 * j + SEG * (1 - c)), :], xb.at[pl.ds(CRECV + 128 * j, 128), :], sib)
+            for j in range(4)
+        )
+        first_in = [
+            bring(s.at[half, :], front4.at[pl.ds(HALF * k, HALF), :]) for k, s in enumerate((after_h, gate_h, n2_h, dh2_h))
+        ]
+        first_in += [bring(adj_h.at[rows(own_at, HALF), :], adj), bring(wg_h, wg), bring(r2_h.at[half, :], r2)]
+        first_in += [bring(wo_h, wo)]
+        second_in = [
+            bring(s.at[half, :], red.at[rows(spot, HALF), :])
+            for s, spot in ((a_h, A), (v_h, V), (sr_h, SR), (w_h, W), (rd_h, RD), (sn_h, SN), (sd_h, SD))
+        ]
+        third_in = [
+            bring(s.at[half, lanes], d)
+            for s, d in (
+                (mixed_h, mixed), (chrec_h, chrec), (keyed_h, keyed), (valued_h, valued), (recepted_h, recepted),
+            )
+        ]
+        third_in += [bring(r1_h.at[half, :], r1), bring(wr_h, wr)]
         for k, v in enumerate(given):
             pv[k : k + 1, :] = v[...].reshape(1, D)
         through[...] = decay_tables(dec[...], rise, fade)
         expu[...] = jnp.exp(rew[...])
         acc[...] = jnp.zeros_like(acc)
-        for copy in first_in:
-            copy.wait()
         yield
         for j in (0, 3, 2, 1):
             e_in = take(j)
@@ -930,6 +930,9 @@
             yield
             e_in.wait_recv()
             links.sent(e_in)
+            if j == 0:
+                for copy in first_in:
+                    copy.wait()
             gate_part(j)
             if j == 0:
                 gsend[...] = fin[SEG : SEG + 8, :]
@@ -1018,10 +1021,14 @@
     jobs = dict(zip("abcd", ffs))
     jobs.update(zip("pqrst", (reduce_weights(k) for k in range(MATS))))
     jobs.update(M=compute(), B=other_half(), V=vectors(), O=result(), G=input_grads())
+    arrived = 0
     for name in "".join(ORDER):
         next(jobs[name], None)
         links.settle(SETTLE)
-    for copy in shared:
+        while shared[arrived:] and shared[arrived][0] < links.step - SETTLE:
+            shared[arrived][1].wait_recv()
+            arrived += 1
+    for _, copy in shared[arrived:]:
         copy.wait_recv()
     links.finish()
 

time: 173 us -> 170 us (0.983)
  Pallas kernels: 172 us -> 169 us
    pallas_call x1, Pallas kernels: 138 us -> 136 us  [back(): pl.pallas_call(back_kernel, in_specs=[pl.BlockSpec(memory_space=pltpu.SME...]
where the time goes in v2:
time: 170 us
  Pallas kernels  169 us (99%)
    pallas_call x1, Pallas kernels, back(): pl.pallas_call(back_kernel, in_specs=[pl.BlockSpec(memory_space=pltpu.SME...  136 us
    pallas_call x1, Pallas kernels, front(): pl.pallas_call(front_kernel, grid_spec=pltpu.PrefetchScalarGridSpec(num_s...  25.6 us
    pallas_call x1, Pallas kernels, finish(): pl.pallas_call(finish_kernel, in_specs=[vmem] * 5, out_specs=[anywhere] *...  7.97 us

profile of v2, /device:TPU:1, one launch (start us, length us, event | category | flops | bytes accessed | tf_op | source)
XLA Modules:
  0.0 170.0 jit_solution(11671038533053235017)
XLA Ops:
  0.7 25.6 %front.1 = (f32[2,16]{1,0:T(2,128)}, f32[2048,768]{1,0:T(8,128)}, f32[1536,768]{1,0:T(8,128)}, f32[512,768]{1,0:T(8,128)}, f32[512,768]{1,0:T(8,128)}, /*index=5...) custom-call(s32[1]{0:T(128)} %bitcast.half_ref, ...), custom_call_target="tpu_custom_call" | custom-call | flops 13287555072 | bytes 62914560 | tf_op jit(solution)/shard_map/front/pallas_call | solution.py:352
  26.3 135.5 %back.1 = (bf16[1024,768]{1,0:T(8,128)(2,1)S(1)}, f32[1024,768]{1,0:T(8,128)S(1)}, f32[16,768]{1,0:T(8,128)S(1)}, f32[4096,768]{1,0:T(8,128)S(1)}, f32[1536,768]{1,0:T(8,128)S(1)}) custom-call(f32[2,16]{1,0:T(2,128)} %get-tuple-element.68.flags, f32[2048,768]{1,0:T(8,128)} %get-tuple-element.69.pq, f32[1536,768]{1,0:T(8,128)} %get-tuple-element.70.grads, ...), custom_call_target="tpu_custom_call" | custom-call | flops 8455716864 | bytes 62914560 | tf_op jit(solution)/shard_map/back/pallas_call | solution.py:1043
  161.8 8.0 %finish.1 = (bf16[1024,768]{1,0:T(8,128)(2,1)}, f32[1024,768]{1,0:T(8,128)}, f32[768,768]{1,0:T(8,128)}, f32[768,768]{1,0:T(8,128)}, f32[768,768]{1,0:T(8,128)},...) custom-call(bf16[1024,768]{1,0:T(8,128)(2,1)S(1)} %get-tuple-element, ...), custom_call_target="tpu_custom_call" | custom-call | tf_op jit(solution)/shard_map/finish/pallas_call | solution.py:1084

commit v3 on v2

--- a/solution.py
+++ b/solution.py
@@ -381,9 +381,9 @@
 SETTLE = 14
 NEAR = (0, 1, 2, 3, 4)
 ORDER = (
-    "daBBacBdaBBdMMbaMMcdBbMdBBacbMdMaMbMcMbcaMMMOMpM",
-    "qMOMMMrMtsMpMqsObMOrMtqpscrqbsOdMtapqOrsMcOtGOpG",
-    "rtVsGrptOqVGrsGGdqGctVbpGtGrspqV",
+    "adBBBadBbcMMdBabcMMadBMbadMBcBMabMcdMMcbaMMMMOMp",
+    "qMMMMrsMtMpqMMtsrOqbpstrqOcMMbsptaMrOdqGstprOsVt",
+    "bGcqGrpVstqrdVpGtcGrsqpV",
 )
 NVEC = 11
 
@@ -997,15 +997,15 @@
 
     def swap(src, src_at, dst, dst_at, back_at):
         there = []
-        for k in range(4):
+        for k in range(2):
             there.append(
-                links.send(src.at[rows(src_at + SEG * k, SEG), :], dst.at[rows(dst_at + SEG * k, SEG), :], opp)
+                links.send(src.at[rows(src_at + 128 * k, 128), :], dst.at[rows(dst_at + 128 * k, 128), :], opp)
             )
             yield
         onward = []
-        for k in range(4):
+        for k in range(2):
             there[k].wait_recv()
-            theirs = dst.at[rows(back_at + SEG * k, SEG), :]
+            theirs = dst.at[rows(back_at + 128 * k, 128), :]
             onward.append(links.send(theirs, theirs, sib))
             yield
         for copy in onward:

time: 170 us -> 170 us (level)
  no operation moved by 1% of the time
where the time goes in v3:
time: 170 us
  Pallas kernels  169 us (99%)
    pallas_call x1, Pallas kernels, back(): pl.pallas_call(back_kernel, in_specs=[pl.BlockSpec(memory_space=pltpu.SME...  136 us
    pallas_call x1, Pallas kernels, front(): pl.pallas_call(front_kernel, grid_spec=pltpu.PrefetchScalarGridSpec(num_s...  25.6 us
    pallas_call x1, Pallas kernels, finish(): pl.pallas_call(finish_kernel, in_specs=[vmem] * 5, out_specs=[anywhere] *...  7.97 us

profile of v3, /device:TPU:1, one launch (start us, length us, event | category | flops | bytes accessed | tf_op | source)
XLA Modules:
  0.0 170.0 jit_solution(2116997882358931801)
XLA Ops:
  0.7 25.6 %front.1 = (f32[2,16]{1,0:T(2,128)}, f32[2048,768]{1,0:T(8,128)}, f32[1536,768]{1,0:T(8,128)}, f32[512,768]{1,0:T(8,128)}, f32[512,768]{1,0:T(8,128)}, /*index=5...) custom-call(s32[1]{0:T(128)} %bitcast.half_ref, ...), custom_call_target="tpu_custom_call" | custom-call | flops 13287555072 | bytes 62914560 | tf_op jit(solution)/shard_map/front/pallas_call | solution.py:352
  26.3 135.5 %back.1 = (bf16[1024,768]{1,0:T(8,128)(2,1)S(1)}, f32[1024,768]{1,0:T(8,128)S(1)}, f32[16,768]{1,0:T(8,128)S(1)}, f32[4096,768]{1,0:T(8,128)S(1)}, f32[1536,768]{1,0:T(8,128)S(1)}) custom-call(f32[2,16]{1,0:T(2,128)} %get-tuple-element.68.flags, f32[2048,768]{1,0:T(8,128)} %get-tuple-element.69.pq, f32[1536,768]{1,0:T(8,128)} %get-tuple-element.70.grads, ...), custom_call_target="tpu_custom_call" | custom-call | flops 8455716864 | bytes 62914560 | tf_op jit(solution)/shard_map/back/pallas_call | solution.py:1043
  161.8 8.0 %finish.1 = (bf16[1024,768]{1,0:T(8,128)(2,1)}, f32[1024,768]{1,0:T(8,128)}, f32[768,768]{1,0:T(8,128)}, f32[768,768]{1,0:T(8,128)}, f32[768,768]{1,0:T(8,128)},...) custom-call(bf16[1024,768]{1,0:T(8,128)(2,1)S(1)} %get-tuple-element, ...), custom_call_target="tpu_custom_call" | custom-call | tf_op jit(solution)/shard_map/finish/pallas_call | solution.py:1084
